TPU v7x, 128 devices: a whole 4x4x4 slice. The times are simulated.
128 devices in a mesh: row: 8 (over z, core), col: 16 (over x, y).
Axes of the slice: x: 4, y: 4, z: 4, core: 2. Of those that a mesh axis runs over, the one named last changes fastest.
Arguments:
- context: bfloat16 [1024, 6144], P('col', 'row'), may hold values from -3 to 3
- residual: bfloat16 [1024, 12288], P('row', 'col'), may hold values from -80 to 80
- norm_gain: float32 [12288], P('col'), may hold values from 0.1 to 1.9
- w_out: bfloat16 [6144, 12288], P('row', 'col'), may hold values from -0.078125 to 0.078125
- w_up: bfloat16 [12288, 24576], P('col', 'row'), may hold values from -4 to 4
- w_down: bfloat16 [24576, 12288], P('row', 'col'), may hold values from -0.0390625 to 0.0390625
- upstream: bfloat16 [1024, 12288], P('row', 'col'), may hold values from -6 to 6
Outputs:
- grad_residual: bfloat16 [1024, 12288], P('row', 'col')
- grad_context: bfloat16 [1024, 6144], P('col', 'row')
- grad_gain: float32 [12288], P('col')
- grad_w_out: bfloat16 [6144, 12288], P('row', 'col')
- grad_w_up: bfloat16 [12288, 24576], P('col', 'row')
- grad_w_down: bfloat16 [24576, 12288], P('row', 'col')
All inputs are finite; a program needn't handle non-finite values.
Results may differ from a plain program's by a relative error of at most 0.029.
Values may be sent and summed in bfloat16 or wider, within the bound.
A program may use at most 128 MiB of HBM per device.

v0:
```python
import jax
import jax.numpy as jnp
from jax import lax
from jax.sharding import PartitionSpec as P

D = 12288


def gelu_value(values):
    tanh_arg = 0.7978845608028654 * (values + 0.044715 * values * values * values)
    return 0.5 * values * (1.0 + jnp.tanh(tanh_arg))


def gelu_slope(values):
    tanh_val = jnp.tanh(0.7978845608028654 * (values + 0.044715 * values * values * values))
    return 0.5 * (1.0 + tanh_val) + 0.5 * values * (
        1.0 - tanh_val * tanh_val
    ) * 0.7978845608028654 * (1.0 + 0.134145 * values * values)


def contract_rows(first_op, second_op):
    return lax.dot_general(
        first_op, second_op, (((0,), (0,)), ((), ())), preferred_element_type=jnp.float32
    )


def contract_cols(first_op, second_op):
    return lax.dot_general(
        first_op, second_op, (((1,), (1,)), ((), ())), preferred_element_type=jnp.float32
    )


def on_device(context, residual, norm_gain, w_out, w_up, w_down, upstream):
    feature_count = float(D)
    context_all = lax.all_gather(context, "col", axis=0, tiled=True)
    attended = lax.psum_scatter(
        jnp.dot(context_all, w_out, preferred_element_type=jnp.float32).astype(jnp.bfloat16),
        "row",
        scatter_dimension=0,
        tiled=True,
    ).astype(jnp.float32)
    summed = residual.astype(jnp.float32) + attended
    row_mean = lax.psum(jnp.sum(summed, axis=1, keepdims=True), "col") / feature_count
    centered = summed - row_mean
    row_var = lax.psum(jnp.sum(centered * centered, axis=1, keepdims=True), "col") / feature_count
    inv_std = lax.rsqrt(row_var + 1e-05)
    unit_rows = centered * inv_std
    normed = (unit_rows * norm_gain).astype(jnp.bfloat16)
    normed_all = lax.all_gather(normed, "row", axis=0, tiled=True)
    upstream_all = lax.all_gather(upstream, "row", axis=0, tiled=True)
    pre_share = lax.psum_scatter(
        jnp.dot(normed_all, w_up, preferred_element_type=jnp.float32).astype(jnp.bfloat16),
        "col",
        scatter_dimension=0,
        tiled=True,
    ).astype(jnp.float32)
    act_share = gelu_value(pre_share).astype(jnp.bfloat16)
    activated = lax.all_gather(act_share, "col", axis=0, tiled=True)
    grad_share = lax.psum_scatter(
        contract_cols(upstream_all, w_down).astype(jnp.bfloat16),
        "col",
        scatter_dimension=0,
        tiled=True,
    ).astype(jnp.float32)
    pre_grad_share = (grad_share * gelu_slope(pre_share)).astype(jnp.bfloat16)
    grad_pre = lax.all_gather(pre_grad_share, "col", axis=0, tiled=True)
    grad_w_down = contract_rows(activated, upstream_all).astype(jnp.bfloat16)
    grad_w_up = contract_rows(normed_all, grad_pre).astype(jnp.bfloat16)
    grad_normed = lax.psum_scatter(
        contract_cols(grad_pre, w_up).astype(jnp.bfloat16), "row", scatter_dimension=0, tiled=True
    ).astype(jnp.float32)
    scaled = grad_normed * norm_gain
    sum_scaled, sum_aligned = lax.psum(
        (
            jnp.sum(scaled, axis=1, keepdims=True),
            jnp.sum(scaled * unit_rows, axis=1, keepdims=True),
        ),
        "col",
    )
    grad_residual = (
        upstream.astype(jnp.float32)
        + inv_std
        * (scaled - sum_scaled / feature_count - unit_rows * (sum_aligned / feature_count))
    ).astype(jnp.bfloat16)
    grad_gain = lax.psum(jnp.sum(grad_normed * unit_rows, axis=0), "row")
    residual_all = lax.all_gather(grad_residual, "row", axis=0, tiled=True)
    grad_w_out = contract_rows(context_all, residual_all).astype(jnp.bfloat16)
    grad_context = lax.psum_scatter(
        contract_cols(residual_all, w_out).astype(jnp.bfloat16),
        "col",
        scatter_dimension=0,
        tiled=True,
    )
    return (grad_residual, grad_context, grad_gain, grad_w_out, grad_w_up, grad_w_down)


def solution(mesh):
    return jax.shard_map(
        on_device,
        mesh=mesh,
        in_specs=(
            P("col", "row"),
            P("row", "col"),
            P("col"),
            P("row", "col"),
            P("col", "row"),
            P("row", "col"),
            P("row", "col"),
        ),
        out_specs=(
            P("row", "col"),
            P("col", "row"),
            P("col"),
            P("row", "col"),
            P("col", "row"),
            P("row", "col"),
        ),
        check_vma=False,
    )
```

profile of v0, /device:TPU:0, one launch (start us, length us, event | category | flops | bytes accessed | tf_op | source)
XLA Modules:
  0.0 675.6 jit_solution(3199500412613483024)
XLA Ops:
  8.0 48.5 %all-gather.7.cloned.1.call-done = bf16[1024,768]{1,0:T(8,128)(2,1)} async-done(((bf16[64,768]{1,0:T(8,128)(2,1)}), bf16[1024,768]{1,0:T(8,128)(2,1)}) %all-gather.7.cloned.1.call-update) | async-done | bytes 1572880 | tf_op jit(solution)/shard_map/all_gather | solution.py:35
  56.5 3.9 convolution_convert_fusion.6
  61.3 31.7 %reduce-scatter.6.cloned.1.call-done = bf16[128,768]{1,0:T(8,128)(2,1)} async-done(((bf16[1024,768]{1,0:T(8,128)(2,1)}), bf16[128,768]{1,0:T(8,128)(2,1)}) %reduce-scatter.6.cloned.1.call-update) | async-done | bytes 196624 | tf_op jit(solution)/shard_map/reduce_scatter | solution.py:36
  94.0 40.3 %psum.35 = f32[128,1]{0,1:T(1,128)S(1)} all-reduce(f32[128,1]{0,1:T(1,128)S(1)} %bitcast.32), channel_id=1, replica_groups=mesh['row'=8,'col'=16] {'col'}, use_global_device_ids=true, to_apply=%region_2.0 | all-reduce | flops 128 | bytes 1024 | tf_op jit(solution)/shard_map/psum | solution.py:43
  135.5 35.5 %psum.36 = f32[128,1]{0,1:T(1,128)S(1)} all-reduce(f32[128,1]{0,1:T(1,128)S(1)} %bitcast.33), channel_id=1, replica_groups=mesh['row'=8,'col'=16] {'col'}, use_global_device_ids=true, to_apply=%region_4.0 | all-reduce | flops 128 | bytes 1024 | tf_op jit(solution)/shard_map/psum | solution.py:45
  172.8 9.2 %convolution_convert_fusion.1 = bf16[1024,3072]{1,0:T(8,128)(2,1)} fusion(bf16[1024,768]{1,0:T(8,128)(2,1)} %all-gather.9.cloned.1.call-done, bf16[3072,768]{1,0:T(8,128)(2,1)} %param.12), kind=kOutput, calls=%fused_computation.1 | convolution fusion | flops 4834983936 | bytes 12582912 | tf_op jit(solution)/shard_map/dot_general | solution.py:28
  182.0 10.6 %all-gather.11.cloned.1.call-done = bf16[1024,768]{1,0:T(8,128)(2,1)} async-done(((bf16[128,768]{1,0:T(8,128)(2,1)}), bf16[1024,768]{1,0:T(8,128)(2,1)}) %all-gather.11.cloned.1.call-update) | async-done | bytes 1572880 | tf_op jit(solution)/shard_map/all_gather | solution.py:49
  192.6 9.0 %convolution_convert_fusion = bf16[1024,3072]{1,0:T(8,128)(2,1)} fusion(bf16[1024,768]{1,0:T(8,128)(2,1)} %all-gather.11.cloned.1.call-done, bf16[768,3072]{1,0:T(8,128)(2,1)} %param.11), kind=kOutput, calls=%fused_computation | convolution fusion | flops 4834983936 | bytes 12582912 | tf_op jit(solution)/shard_map/dot_general | solution.py:52
  201.8 75.5 %reduce-scatter.8.cloned.1.call-done = bf16[64,3072]{1,0:T(8,128)(2,1)} async-done(((bf16[1024,3072]{1,0:T(8,128)(2,1)}), bf16[64,3072]{1,0:T(8,128)(2,1)}) %reduce-scatter.8.cloned.1.call-update) | async-done | bytes 393232 | tf_op jit(solution)/shard_map/reduce_scatter | solution.py:59
  277.2 83.9 %reduce-scatter.10.cloned.1.call-done = bf16[64,3072]{1,0:T(8,128)(2,1)} async-done(((bf16[1024,3072]{1,0:T(8,128)(2,1)}), bf16[64,3072]{1,0:T(8,128)(2,1)}) %reduce-scatter.10.cloned.1.call-update) | async-done | bytes 393232 | tf_op jit(solution)/shard_map/reduce_scatter | solution.py:51
  361.2 2.6 fusion.8
  363.8 60.7 %all-gather.13.cloned.1.call-done = bf16[1024,3072]{1,0:T(8,128)(2,1)} async-done(((bf16[64,3072]{1,0:T(8,128)(2,1)}), bf16[1024,3072]{1,0:T(8,128)(2,1)}) %all-gather.13.cloned.1.call-update) | async-done | bytes 6291472 | tf_op jit(solution)/shard_map/all_gather | solution.py:66
  424.5 9.5 %convolution_convert_fusion.5 = bf16[1024,768]{1,0:T(8,128)(2,1)} fusion(bf16[1024,3072]{1,0:T(8,128)(2,1)} %all-gather.13.cloned.1.call-done, bf16[768,3072]{1,0:T(8,128)(2,1)} %param.11), kind=kOutput, calls=%fused_computation.12 | convolution fusion | flops 4832624640 | bytes 12582912 | tf_op jit(solution)/shard_map/dot_general | solution.py:28
  434.1 32.8 %reduce-scatter.12.cloned.1.call-done = bf16[128,768]{1,0:T(8,128)(2,1)} async-done(((bf16[1024,768]{1,0:T(8,128)(2,1)}), bf16[128,768]{1,0:T(8,128)(2,1)}) %reduce-scatter.12.cloned.1.call-update) | async-done | bytes 196624 | tf_op jit(solution)/shard_map/reduce_scatter | solution.py:69
  468.0 40.2 %all-reduce = (f32[128,1]{0,1:T(1,128)S(1)}, f32[128,1]{0,1:T(1,128)S(1)}) all-reduce(f32[128,1]{0,1:T(1,128)S(1)} %bitcast.30, f32[128,1]{0,1:T(1,128)S(1)} %bitcast.31), channel_id=1, replica_groups=mesh['row'=8,'col'=16] {'col'}, use_global_device_ids=true, to_apply=%region_11.0 | all-reduce | flops 256 | bytes 2048 | tf_op jit(solution)/shard_map/psum | solution.py:73
  508.3 1.8 fusion.18
  510.9 17.2 %all-gather.15.cloned.1.call-done = bf16[1024,768]{1,0:T(8,128)(2,1)} async-done(((bf16[128,768]{1,0:T(8,128)(2,1)}), bf16[1024,768]{1,0:T(8,128)(2,1)}) %all-gather.15.cloned.1.call-update) | async-done | bytes 1572880 | tf_op jit(solution)/shard_map/all_gather | solution.py:86
  528.1 4.0 convolution_convert_fusion.4
  532.2 9.2 %convolution_convert_fusion.3 = bf16[768,3072]{1,0:T(8,128)(2,1)} fusion(bf16[1024,768]{1,0:T(8,128)(2,1)} %all-gather.11.cloned.1.call-done, bf16[1024,3072]{1,0:T(8,128)(2,1)} %all-gather.13.cloned.1.call-done), kind=kOutput, calls=%fused_computation.3 | convolution fusion | flops 4834197504 | bytes 12582912 | tf_op jit(solution)/shard_map/dot_general | solution.py:22
  541.4 50.7 %all-gather.17.cloned.1.call-done = bf16[1024,3072]{1,0:T(8,128)(2,1)} async-done(((bf16[64,3072]{1,0:T(8,128)(2,1)}), bf16[1024,3072]{1,0:T(8,128)(2,1)}) %all-gather.17.cloned.1.call-update) | async-done | bytes 6291472 | tf_op jit(solution)/shard_map/all_gather | solution.py:58
  592.1 9.6 %convolution_convert_fusion.2 = bf16[3072,768]{1,0:T(8,128)(2,1)} fusion(bf16[1024,3072]{1,0:T(8,128)(2,1)} %all-gather.17.cloned.1.call-done, bf16[1024,768]{1,0:T(8,128)(2,1)S(1)} %copy-done.5), kind=kOutput, calls=%fused_computation.2 | convolution fusion | flops 4834197504 | bytes 12582912 | tf_op jit(solution)/shard_map/dot_general | solution.py:22
  601.7 15.4 %psum.39 = f32[768]{0:T(1024)} all-reduce(f32[768]{0:T(1024)S(1)} %get-tuple-element.12), channel_id=1, replica_groups=mesh['row'=8,'col'=16] {'row'}, use_global_device_ids=true, to_apply=%region_14.0 | all-reduce | flops 768 | bytes 6144 | tf_op jit(solution)/shard_map/psum | solution.py:85
  617.1 3.4 fusion
  621.9 47.2 %reduce-scatter.14.cloned.1.call-done = bf16[64,768]{1,0:T(8,128)(2,1)} async-done(((bf16[1024,768]{1,0:T(8,128)(2,1)}), bf16[64,768]{1,0:T(8,128)(2,1)}) %reduce-scatter.14.cloned.1.call-update) | async-done | bytes 98320 | tf_op jit(solution)/shard_map/reduce_scatter | solution.py:88
  (43 shorter events, 9.3 us)
Async XLA Ops:
  7.2 49.3 %copy-start = (bf16[768,768]{1,0:T(8,128)(2,1)S(1)}, bf16[768,768]{1,0:T(8,128)(2,1)}, u32[]{:S(2)}) copy-start(bf16[768,768]{1,0:T(8,128)(2,1)} %param.10) | copy-start | bytes 3538948
  7.2 49.3 %all-gather.7.cloned.1.call-start = ((), (), s32[]{:S(2)}) async-start(), calls=%async_computation.5 | async-start | bytes 1671168 | tf_op jit(solution)/shard_map/all_gather | solution.py:35
  7.9 85.0 %reduce-scatter.6.cloned.1.call-start = ((), (), s32[]{:S(2)}) async-start(), calls=%async_computation.6 | async-start | bytes 1769472 | tf_op jit(solution)/shard_map/reduce_scatter | solution.py:36
  60.4 32.5 %copy-start.1 = (bf16[128,768]{1,0:T(8,128)(2,1)S(1)}, bf16[128,768]{1,0:T(8,128)(2,1)}, u32[]{:S(2)}) copy-start(bf16[128,768]{1,0:T(8,128)(2,1)} %param.8) | copy-start | bytes 589828
  60.4 110.5 %copy-start.4 = (f32[768]{0:T(1024)S(1)}, f32[768]{0:T(1024)}, u32[]{:S(2)}) copy-start(f32[768]{0:T(1024)} %param.9) | copy-start | bytes 9220
  60.5 112.3 %all-gather.9.cloned.1.call-start = ((), (), s32[]{:S(2)}) async-start(), calls=%async_computation.7 | async-start | bytes 1769472 | tf_op jit(solution)/shard_map/all_gather | solution.py:50
  61.2 131.4 %all-gather.11.cloned.1.call-start = ((), (), s32[]{:S(2)}) async-start(), calls=%async_computation.9 | async-start | bytes 1769472 | tf_op jit(solution)/shard_map/all_gather | solution.py:49
  172.7 104.5 %reduce-scatter.8.cloned.1.call-start = ((), (), s32[]{:S(2)}) async-start(), calls=%async_computation.8 | async-start | bytes 6684672 | tf_op jit(solution)/shard_map/reduce_scatter | solution.py:59
  182.0 179.2 %reduce-scatter.10.cloned.1.call-start = ((), (), s32[]{:S(2)}) async-start(), calls=%async_computation.10 | async-start | bytes 6684672 | tf_op jit(solution)/shard_map/reduce_scatter | solution.py:51
  201.7 222.8 %all-gather.13.cloned.1.call-start = ((), (), s32[]{:S(2)}) async-start(), calls=%async_computation.11 | async-start | bytes 6684672 | tf_op jit(solution)/shard_map/all_gather | solution.py:66
  363.8 103.1 %reduce-scatter.12.cloned.1.call-start = ((), (), s32[]{:S(2)}) async-start(), calls=%async_computation.12 | async-start | bytes 1769472 | tf_op jit(solution)/shard_map/reduce_scatter | solution.py:69
  434.0 32.8 %copy-start.2 = (bf16[128,768]{1,0:T(8,128)(2,1)S(1)}, bf16[128,768]{1,0:T(8,128)(2,1)}, u32[]{:S(2)}) copy-start(bf16[128,768]{1,0:T(8,128)(2,1)} %reduce-scatter.6.cloned.1.call-done) | copy-start | bytes 589828
  434.0 74.3 %copy-start.3 = (bf16[128,768]{1,0:T(8,128)(2,1)S(1)}, bf16[128,768]{1,0:T(8,128)(2,1)}, u32[]{:S(2)}) copy-start(bf16[128,768]{1,0:T(8,128)(2,1)} %param.13) | copy-start | bytes 589828
  434.0 94.1 %all-gather.15.cloned.1.call-start = ((), (), s32[]{:S(2)}) async-start(), calls=%async_computation.13 | async-start | bytes 1769472 | tf_op jit(solution)/shard_map/all_gather | solution.py:86
  510.1 82.0 %all-gather.17.cloned.1.call-start = ((), (), s32[]{:S(2)}) async-start(), calls=%async_computation.15 | async-start | bytes 6684672 | tf_op jit(solution)/shard_map/all_gather | solution.py:58
  510.7 158.4 %reduce-scatter.14.cloned.1.call-start = ((), (), s32[]{:S(2)}) async-start(), calls=%async_computation.14 | async-start | bytes 1671168 | tf_op jit(solution)/shard_map/reduce_scatter | solution.py:88
  532.2 59.9 %copy-start.5 = (bf16[1024,768]{1,0:T(8,128)(2,1)S(1)}, bf16[1024,768]{1,0:T(8,128)(2,1)}, u32[]{:S(2)}) copy-start(bf16[1024,768]{1,0:T(8,128)(2,1)} %all-gather.9.cloned.1.call-done) | copy-start | bytes 4718596
Sparse Core Ops, SparseCore 0:
  10.2 46.2 all-gather.6
  60.6 32.2 reduce-scatter.5
  94.6 23.1 all-gather.8
  172.8 19.7 all-gather.10
  195.9 81.2 reduce-scatter.7
  280.5 80.5 reduce-scatter.9
  363.9 60.5 all-gather.12
  434.2 32.6 reduce-scatter.11
  510.2 17.8 all-gather.14
  530.8 61.2 all-gather.16
  595.9 73.1 reduce-scatter.13
where the time goes:
time: 676 us
  waiting for transfers between devices  461 us (68%)
  blocking collectives  131 us (19%)
  matrix products  57.8 us (9%)
  between operations  13.9 us (2%)
  other arithmetic  9.5 us (1%)
    reduce_scatter x1, waiting for transfers between devices, on_device(): lax.psum_scatter(jnp.dot(normed_all, w_up, preferred_element_type=jnp.flo...  83.9 us
    reduce_scatter x1, waiting for transfers between devices, on_device(): lax.psum_scatter(contract_cols(upstream_all, w_down).astype(jnp.bfloat16)...  75.5 us
    all_gather x1, waiting for transfers between devices, on_device(): grad_pre = lax.all_gather(pre_grad_share, 'col', axis=0, tiled=True)  60.7 us
    all_gather x1, waiting for transfers between devices, on_device(): activated = lax.all_gather(act_share, 'col', axis=0, tiled=True)  50.7 us
    all_gather x1, waiting for transfers between devices, on_device(): context_all = lax.all_gather(context, 'col', axis=0, tiled=True)  48.5 us
    reduce_scatter x1, waiting for transfers between devices, on_device(): lax.psum_scatter(contract_cols(residual_all, w_out).astype(jnp.bfloat16),...  47.2 us
    psum x1, blocking collectives, on_device(): lax.psum(jnp.sum(summed, axis=1, keepdims=True), 'col') / feature_count  40.3 us
    psum x1, blocking collectives, on_device(): lax.psum((jnp.sum(scaled, axis=1, keepdims=True), jnp.sum(scaled * unit_r...  40.2 us
  transfers between devices with their start and end apart: 11, of which 10 were waited for; matrix products, arithmetic and copies ran while one was open for 7% of the time, Pallas kernels for 0%

commit v1 on v0

v1 whole, which is shorter than its diff:
```python
import jax
import jax.numpy as jnp
from jax import lax
from jax.experimental import pallas as pl
from jax.experimental.pallas import tpu as pltpu
from jax.sharding import PartitionSpec as P

MESH = pl.DeviceIdType.MESH
BF16 = jnp.bfloat16
F32 = jnp.float32
D = 12288
W = 768
PAIRS = 6
C = 256
CH = 384
ACT_DELAY = 6
TICKS = 28


def gelu_parts(values):
    tanh_val = jnp.tanh(0.7978845608028654 * (values + 0.044715 * values * values * values))
    value = 0.5 * values * (1.0 + tanh_val)
    slope = 0.5 * (1.0 + tanh_val) + 0.5 * values * (
        1.0 - tanh_val * tanh_val
    ) * 0.7978845608028654 * (1.0 + 0.134145 * values * values)
    return value, slope


def dot(first_op, second_op):
    return jnp.dot(first_op, second_op, preferred_element_type=F32)


def dot_cols(first_op, second_op):
    return lax.dot_general(
        first_op, second_op, (((1,), (1,)), ((), ())), preferred_element_type=F32
    )


class Ring:
    def __init__(self, place, device):
        self.place = place
        self.right = lax.rem(place + 1, 4)
        self.opposite = lax.rem(place + 2, 4)
        self.left = lax.rem(place + 3, 4)
        self.device = device


def remote(src, dst, send, recv, device):
    return pltpu.make_async_remote_copy(
        src_ref=src, dst_ref=dst, send_sem=send, recv_sem=recv, device_id=device, device_id_type=MESH
    )


class Copies:
    def __init__(self, make, count):
        self.make, self.count = make, count

    def __getitem__(self, k):
        return self.make(k)

    def __iter__(self):
        return (self.make(k) for k in range(self.count))


class Scatter:
    def __init__(self, ring, half, landing, send, recv):
        r, l, o = ring.right, ring.left, ring.opposite
        plan = [(o, 0, r), (r, 1, r), (r, 0, r), (o, 1, l), (l, 0, l), (l, 1, l)]
        self.ring, self.half, self.landing = ring, half, landing

        def make(k):
            i, h, to = plan[k]
            return remote(half(i, h), landing.at[k], send.at[k], recv.at[k], ring.device(to))

        self.copies = Copies(make, 6)

    def start(self):
        for k in (0, 3, 1, 4):
            self.copies[k].start()

    def middle(self):
        for k, i, h, nxt in ((0, self.ring.right, 0, 2), (3, self.ring.left, 1, 5)):
            self.copies[k].wait_recv()
            part = self.half(i, h)
            part[...] = (part[...].astype(F32) + self.landing[k].astype(F32)).astype(BF16)
            self.copies[nxt].start()

    def finish(self):
        for k in (1, 4, 2, 5):
            self.copies[k].wait_recv()
        for copy in self.copies:
            copy.wait_send()
        me = self.ring.place
        first = (
            self.half(me, 0)[...].astype(F32)
            + self.landing[2].astype(F32)
            + self.landing[4].astype(F32)
        )
        second = (
            self.half(me, 1)[...].astype(F32)
            + self.landing[1].astype(F32)
            + self.landing[5].astype(F32)
        )
        return first, second


class Gather:
    def __init__(self, ring, group, half, send, recv):
        r, l = ring.right, ring.left
        me = ring.place

        def make(k):
            ref = (lambda: group(me), lambda: group(me), lambda: half(l, 0), lambda: half(r, 1))[k]()
            return remote(ref, ref, send.at[k], recv.at[k], ring.device((r, l, r, l)[k]))

        self.copies = Copies(make, 4)

    def start(self):
        self.copies[0].start()
        self.copies[1].start()

    def middle(self):
        self.copies[0].wait_recv()
        self.copies[2].start()
        self.copies[1].wait_recv()
        self.copies[3].start()

    def arrived(self):
        self.copies[2].wait_recv()
        self.copies[3].wait_recv()

    def sent(self):
        for copy in self.copies:
            copy.wait_send()


def grouped(ref, order, i, low, count):
    if order == 0:
        return ref.at[i, pl.ds(low, count)]
    return ref.at[pl.ds(low, count), i]


def block_of(ref, order, i, j):
    return ref.at[i, j] if order == 0 else ref.at[j, i]


def kernel(
    ctx_in, res_in, gain_in, w_out_in, w_up_hbm, w_down_hbm, ups_in,
    res_out, ctx_out, gain_out, w_out_out, w_up_out, w_down_out,
    w_up, w_down, part, land1, land2, act_grad, pre_grad, act,
    ctx_all, ctx_part, ctx_land1, ctx_land2, ups_all, normed_all, res_all, normed_t, total,
    z_part, z_sib, z_land, stat_x, stat_y, unit, inv, gain_sib, gain_z, up_stage, down_stage, act_t,
    w_sem, s1, v1, s2, v2, gs, gv, asend, arecv, cs, cv, c1s, c1v, c2s, c2v,
    zgs, zgv, zss, zsv, sts, stv, ggs, ggv, out_sem,
):
    row, col = lax.axis_index("row"), lax.axis_index("col")
    z, core = row // 2, lax.rem(row, 2)
    x, y = col // 4, lax.rem(col, 4)
    ring_x = Ring(x, lambda i: {"col": i * 4 + y})
    ring_y = Ring(y, lambda i: {"col": x * 4 + i})
    ring_z = Ring(z, lambda i: {"row": i * 2 + core})
    sibling = {"row": z * 2 + 1 - core}
    rings = (ring_x, ring_y)

    load_down = pltpu.make_async_copy(w_down_hbm, w_down, w_sem.at[0])
    load_up = pltpu.make_async_copy(w_up_hbm, w_up, w_sem.at[1])
    load_down.start()
    load_up.start()

    barrier = pltpu.get_barrier_semaphore()
    for ring in (ring_x, ring_y, ring_z):
        for i in (ring.left, ring.right, ring.opposite):
            pl.semaphore_signal(barrier, inc=1, device_id=ring.device(i), device_id_type=MESH)
    pl.semaphore_signal(barrier, inc=1, device_id=sibling, device_id_type=MESH)
    pl.semaphore_wait(barrier, 10)

    def scatter1(ref, landing, send, recv, order):
        ring = rings[order]
        return Scatter(ring, lambda i, h: grouped(ref, order, i, 2 * h, 2), landing, send, recv)

    def scatter2(ref, landing, send, recv, order, rows):
        mine, ring = rings[order].place, rings[1 - order]
        return Scatter(
            ring,
            lambda j, h: block_of(ref, order, mine, j).at[pl.ds(h * rows, rows)],
            landing, send, recv,
        )

    def gather1(ref, send, recv, order):
        mine, ring = rings[order].place, rings[1 - order]
        return Gather(
            ring,
            lambda j: block_of(ref, order, mine, j),
            lambda j, h: block_of(ref, order, mine, j).at[pl.ds(h * 32, 32)],
            send.at[pl.ds(0, 4)], recv.at[pl.ds(0, 4)],
        )

    def gather2(ref, send, recv, order):
        return Gather(
            rings[order],
            lambda i: grouped(ref, order, i, 0, 4),
            lambda i, h: grouped(ref, order, i, 2 * h, 2),
            send.at[pl.ds(4, 4)], recv.at[pl.ds(4, 4)],
        )

    def scatter_turn(ref, landing, send, recv, order):
        one = scatter1(ref, landing, send, recv, order)
        first, second = one.finish()
        one.half(one.ring.place, 0)[...] = first.astype(BF16)
        one.half(one.ring.place, 1)[...] = second.astype(BF16)

    class RowGather:
        def __init__(self, ref, n):
            self.ring = Gather(
                ring_z,
                lambda i: ref.at[i, core],
                lambda i, h: ref.at[i, core, pl.ds(h * 64, 64)],
                zgs.at[n, pl.ds(0, 4)], zgv.at[n, pl.ds(0, 4)],
            )
            blocks = (z, ring_z.left, ring_z.right, ring_z.opposite)
            self.near = Copies(
                lambda k: remote(
                    ref.at[blocks[k], core], ref.at[blocks[k], core],
                    zgs.at[n, 4 + k], zgv.at[n, 4 + k], sibling,
                ),
                4,
            )

        def start(self):
            self.ring.start()
            self.near[0].start()

        def middle(self):
            self.ring.middle()
            self.near[1].start()
            self.near[2].start()

        def last(self):
            self.ring.arrived()
            self.near[3].start()

        def finish(self):
            for copy in self.near:
                copy.wait_recv()
            for copy in self.near:
                copy.wait_send()
            self.ring.sent()

    def row_near():
        return remote(z_part.at[:, 1 - core], z_sib, zss.at[6], zsv.at[6], sibling)

    row_ring = Scatter(
        ring_z, lambda i, h: z_part.at[i, core, pl.ds(h * 64, 64)], z_land, zss, zsv
    )

    def row_scatter_ring():
        row_near().wait_recv()
        row_near().wait_send()
        z_part[:, core] = (z_part[:, core].astype(F32) + z_sib[...].astype(F32)).astype(BF16)
        row_ring.start()

    def stat_copies(n, ref, ring):
        base = 0 if ref is stat_x else 3
        return Copies(
            lambda d: remote(
                ref.at[n, ring.place], ref.at[n, ring.place],
                sts.at[n, base + d], stv.at[n, base + d],
                ring.device(lax.rem(ring.place + 1 + d, 4)),
            ),
            3,
        )

    def to_lanes(first, second):
        lane = lax.broadcasted_iota(jnp.int32, (128, 128), 1)
        both = jnp.where(lane == 0, first, jnp.where(lane == 1, second, 0.0))
        return jnp.transpose(both)[0:8]

    def to_rows(values):
        return jnp.transpose(jnp.broadcast_to(values, (128, 128)))[:, 0:1]

    def stat_start(n, ref, ring, values):
        ref[n, ring.place] = values
        for copy in stat_copies(n, ref, ring):
            copy.start()

    def stat_wait(n, ref, ring):
        for copy in stat_copies(n, ref, ring):
            copy.wait_recv()
        for copy in stat_copies(n, ref, ring):
            copy.wait_send()

    def merge_moments(ref, count):
        means = [ref[0, i, 0:1] for i in range(4)]
        mean = (means[0] + means[1] + means[2] + means[3]) * 0.25
        squares = ref[0, 0, 1:2] + ref[0, 1, 1:2] + ref[0, 2, 1:2] + ref[0, 3, 1:2]
        for one in means:
            squares += count * (one - mean) * (one - mean)
        return mean, squares

    def two_rows(first, second):
        line = lax.broadcasted_iota(jnp.int32, (8, 128), 0)
        return jnp.where(line == 0, first, jnp.where(line == 1, second, 0.0))

    ups_gather, normed_gather, res_gather = (
        RowGather(ref, n) for n, ref in enumerate((ups_all, normed_all, res_all))
    )

    def project_out():
        @pl.loop(0, 4)
        def _(m):
            value = dot(ctx_all[0, m].reshape(256, CH), w_out_in[0:CH, :]) + dot(
                ctx_all[1, m].reshape(256, CH), w_out_in[CH:W, :]
            )
            z_part[m] = value.astype(BF16).reshape(2, 128, W)

        row_near().start()

    def row_moments():
        first, second = row_ring.finish()
        for h, share in enumerate((first, second)):
            unit[pl.ds(h * 64, 64)] = share + res_in[pl.ds(h * 64, 64)].astype(F32)
        summed = unit[...]
        mean = jnp.sum(summed, axis=1, keepdims=True) * (1.0 / W)
        centered = summed - mean
        squares = jnp.sum(centered * centered, axis=1, keepdims=True)
        stat_start(0, stat_x, ring_x, to_lanes(mean, squares))

    def moments_x():
        stat_wait(0, stat_x, ring_x)
        stat_start(0, stat_y, ring_y, two_rows(*merge_moments(stat_x, float(W))))

    def normalize():
        stat_wait(0, stat_y, ring_y)
        mean, squares = merge_moments(stat_y, float(4 * W))
        inv_row = lax.rsqrt(squares * (1.0 / D) + 1e-05)
        inv_std = to_rows(inv_row)
        inv[...] = jnp.broadcast_to(inv_std, (128, 128))
        rows = (unit[...] - to_rows(mean)) * inv_std
        unit[...] = rows
        normed_all[z, core] = (rows * gain_in[...]).astype(BF16)
        normed_gather.start()

    def normed_done():
        normed_gather.finish()
        load_up.wait()

        @pl.loop(0, 4)
        def _(m):
            for c in range(2):
                tokens = pl.ds(pl.multiple_of((m * 2 + c) * 128, 128), 128)
                normed_t[:, tokens] = jnp.transpose(normed_all[m, c])

    def unit_scatter1(i, order):
        slot = lax.rem(i, PAIRS)
        return (
            part.at[slot, order], land1.at[slot, order], s1.at[slot, order], v1.at[slot, order], order
        )

    def unit_scatter2(i, order):
        slot = lax.rem(i, PAIRS)
        return (
            part.at[slot, order], land2.at[slot, order], s2.at[slot, order], v2.at[slot, order], order, 32
        )

    def columns(p, order):
        return pl.ds(pl.multiple_of((p * 2 + order) * C, C), C)

    def multiply(i):
        slot = lax.rem(i, PAIRS)

        @pl.when(i < PAIRS)
        def _():
            for order in range(2):

                @pl.loop(0, 4)
                def _(m):
                    value = dot_cols(ups_all[m].reshape(256, W), w_down[columns(i, order), :])
                    part[slot, order, m] = value.astype(BF16).reshape(4, 64, C)

                scatter1(*unit_scatter1(i, order)).start()

        @pl.when(i >= PAIRS)
        def _():
            for order in range(2):

                @pl.loop(0, 4)
                def _(m):
                    value = dot(normed_all[m].reshape(256, W), w_up[:, columns(i - PAIRS, order)])
                    part[slot, order, m] = value.astype(BF16).reshape(4, 64, C)

                scatter1(*unit_scatter1(i, order)).start()

    def scatter1_middle(i):
        for order in range(2):
            scatter1(*unit_scatter1(i, order)).middle()

    def scatter1_finish(i):
        for order in range(2):
            scatter_turn(*unit_scatter1(i, order))
            scatter2(*unit_scatter2(i, order)).start()

    def scatter2_middle(i):
        for order in range(2):
            scatter2(*unit_scatter2(i, order)).middle()

    def pre_gather(p, order, stage):
        return (gather1, gather2)[stage](
            pre_grad.at[p, order], gs.at[p, order], gv.at[p, order], order
        )

    def act_gather(p, order, stage):
        return (gather1, gather2)[stage](
            act.at[p, order], asend.at[p, order], arecv.at[p, order], order
        )

    def scatter2_finish(i):
        slot = lax.rem(i, PAIRS)
        for order in range(2):
            halves = scatter2(*unit_scatter2(i, order)).finish()

            @pl.when(i < PAIRS)
            def _():
                for h in range(2):
                    act_grad[slot, order, pl.ds(h * 32, 32)] = halves[h]

            @pl.when(i >= PAIRS)
            def _():
                for h in range(2):
                    value, slope = gelu_parts(halves[h])
                    grad = act_grad[slot, order, pl.ds(h * 32, 32)] * slope
                    act[slot, order, x, y, pl.ds(h * 32, 32)] = value.astype(BF16)
                    pre_grad[slot, order, x, y, pl.ds(h * 32, 32)] = grad.astype(BF16)
                pre_gather(slot, order, 0).start()

    def gather_steps(make):
        def start(p):
            for order in range(2):
                make(p, order, 0).start()

        def middle1(p):
            for order in range(2):
                make(p, order, 0).middle()

        def turn(p):
            for order in range(2):
                one = make(p, order, 0)
                one.arrived()
                one.sent()
                make(p, order, 1).start()

        def middle2(p):
            for order in range(2):
                make(p, order, 1).middle()

        def finish(p):
            for order in range(2):
                one = make(p, order, 1)
                one.arrived()
                one.sent()

        return start, middle1, turn, middle2, finish

    _, pre_middle1, pre_turn, pre_middle2, pre_finish = gather_steps(pre_gather)
    act_start, act_middle1, act_turn, act_middle2, act_finish = gather_steps(act_gather)

    def up_store(p, order):
        slot = lax.rem(p, 2)
        return pltpu.make_async_copy(
            up_stage.at[slot, order], w_up_out.at[:, columns(p, order)], out_sem.at[0, slot, order]
        )

    def down_store(p, order):
        slot = lax.rem(p, 2)
        return pltpu.make_async_copy(
            down_stage.at[slot, order], w_down_out.at[columns(p, order), :], out_sem.at[1, slot, order]
        )

    def pre_products(p):
        slot = lax.rem(p, 2)
        for order in range(2):

            @pl.when(p >= 2)
            def _():
                up_store(p - 2, order).wait()

            @pl.loop(0, 3)
            def _(n):
                rows = pl.ds(pl.multiple_of(n * 256, 256), 256)
                value = dot(normed_t[rows, :], pre_grad[p, order].reshape(1024, C))
                up_stage[slot, order, rows, :] = value.astype(BF16)

            up_store(p, order).start()

        @pl.loop(0, 4)
        def _(m):
            value = dot_cols(pre_grad[p, 0, m].reshape(256, C), w_up[:, columns(p, 0)]) + dot_cols(
                pre_grad[p, 1, m].reshape(256, C), w_up[:, columns(p, 1)]
            )
            value = value.reshape(2, 128, W)

            @pl.when(p == 0)
            def _():
                total[m] = value

            @pl.when(p > 0)
            def _():
                total[m] += value

    def act_products(p):
        slot = lax.rem(p, 2)
        for order in range(2):

            @pl.when(p >= 2)
            def _():
                down_store(p - 2, order).wait()

            for m in range(4):
                act_t[:, pl.ds(m * 256, 256)] = jnp.transpose(act[p, order, m].reshape(256, C))

            @pl.loop(0, 3)
            def _(n):
                cols = pl.ds(pl.multiple_of(n * 256, 256), 256)
                value = dot(act_t[...], ups_all[:, :, :, cols].reshape(1024, 256))
                down_stage[slot, order, :, cols] = value.astype(BF16)

            down_store(p, order).start()

    def reduce_rows():
        z_part[...] = total[...].astype(BF16)
        row_near().start()

    def gain_near():
        return remote(gain_sib.at[0], gain_sib.at[1], ggs.at[0], ggv.at[0], sibling)

    gain_far = Copies(
        lambda d: remote(
            gain_z.at[z], gain_z.at[z], ggs.at[1 + d], ggv.at[1 + d],
            ring_z.device(lax.rem(z + 1 + d, 4)),
        ),
        3,
    )

    def grad_sums():
        first, second = row_ring.finish()
        for h, share in enumerate((first, second)):
            total[0, 0, pl.ds(h * 64, 64)] = share
        grad = total[0, 0]
        aligned = grad * unit[...]
        scaled = grad * gain_in[...]
        stat_start(
            1, stat_x, ring_x,
            to_lanes(
                jnp.sum(scaled, axis=1, keepdims=True),
                jnp.sum(scaled * unit[...], axis=1, keepdims=True),
            ),
        )
        gain_sib[0] = jnp.broadcast_to(jnp.sum(aligned, axis=0, keepdims=True), (8, W))
        gain_near().start()

    def sums_x():
        stat_wait(1, stat_x, ring_x)
        stat_start(
            1, stat_y, ring_y, stat_x[1, 0] + stat_x[1, 1] + stat_x[1, 2] + stat_x[1, 3]
        )
        gain_near().wait_recv()
        gain_near().wait_send()
        gain_z[z] = gain_sib[0] + gain_sib[1]
        for copy in gain_far:
            copy.start()

    def grad_rows():
        stat_wait(1, stat_y, ring_y)
        means = (stat_y[1, 0] + stat_y[1, 1] + stat_y[1, 2] + stat_y[1, 3]) * (1.0 / D)
        scaled = total[0, 0] * gain_in[...]
        value = ups_in[...].astype(F32) + inv[:, 0:1] * (
            scaled - to_rows(means[0:1]) - unit[...] * to_rows(means[1:2])
        )
        rounded = value.astype(BF16)
        res_out[...] = rounded
        res_all[z, core] = rounded
        res_gather.start()

    def gain_done():
        for copy in gain_far:
            copy.wait_recv()
        for copy in gain_far:
            copy.wait_send()
        gain_out[...] = gain_z[0] + gain_z[1] + gain_z[2] + gain_z[3]

    def ctx_scatter1(order):
        return ctx_part.at[order], ctx_land1.at[order], c1s.at[order], c1v.at[order], order

    def ctx_scatter2(order):
        return ctx_part.at[order], ctx_land2.at[order], c2s.at[order], c2v.at[order], order, 32

    def context_product():
        res_gather.finish()
        for order in range(2):

            @pl.loop(0, 4)
            def _(m):
                value = dot_cols(
                    res_all[m].reshape(256, W), w_out_in[pl.ds(order * CH, CH), :]
                )
                ctx_part[order, m] = value.astype(BF16).reshape(4, 64, CH)

            scatter1(*ctx_scatter1(order)).start()

    def context_middle1():
        for order in range(2):
            scatter1(*ctx_scatter1(order)).middle()

    def context_turn():
        for order in range(2):
            scatter_turn(*ctx_scatter1(order))
            scatter2(*ctx_scatter2(order)).start()

    def context_middle2():
        for order in range(2):
            scatter2(*ctx_scatter2(order)).middle()

    def context_finish():
        for order in range(2):
            for h, share in enumerate(scatter2(*ctx_scatter2(order)).finish()):
                ctx_out[pl.ds(h * 32, 32), pl.ds(order * CH, CH)] = share.astype(BF16)

    def out_product():
        for order in range(2):
            for n in range(3):
                cols = pl.ds(n * 256, 256)
                value = lax.dot_general(
                    ctx_all[order].reshape(1024, CH),
                    res_all[:, :, :, cols].reshape(1024, 256),
                    (((0,), (0,)), ((), ())),
                    preferred_element_type=F32,
                )
                w_out_out[pl.ds(order * CH, CH), cols] = value.astype(BF16)

    ups_all[z, core] = ups_in[...]
    ups_gather.start()
    for order in range(2):
        ctx_all[order, x, y] = ctx_in[:, pl.ds(order * CH, CH)]
        gather1(ctx_all.at[order], cs.at[order], cv.at[order], order).start()
    for order in range(2):
        gather1(ctx_all.at[order], cs.at[order], cv.at[order], order).middle()
    ups_gather.middle()
    for order in range(2):
        one = gather1(ctx_all.at[order], cs.at[order], cv.at[order], order)
        one.arrived()
        one.sent()
        gather2(ctx_all.at[order], cs.at[order], cv.at[order], order).start()
    ups_gather.last()
    for order in range(2):
        gather2(ctx_all.at[order], cs.at[order], cv.at[order], order).middle()
    ups_gather.finish()
    load_down.wait()

    def context_arrived():
        for order in range(2):
            one = gather2(ctx_all.at[order], cs.at[order], cv.at[order], order)
            one.arrived()
            one.sent()
        project_out()

    early = {
        1: [row_scatter_ring],
        2: [row_moments],
        3: [normalize],
        4: [normed_gather.middle],
        5: [normed_gather.last],
        6: [normed_done],
        20: [row_scatter_ring],
        21: [grad_sums],
        22: [grad_rows],
        23: [res_gather.last],
        24: [context_middle1],
        25: [context_turn],
        26: [context_middle2],
        27: [context_finish],
    }
    late = {
        0: [context_arrived],
        1: [row_ring.middle],
        2: [moments_x],
        19: [reduce_rows],
        20: [row_ring.middle],
        21: [sums_x],
        22: [gain_done, res_gather.middle],
        23: [context_product],
        24: [out_product],
    }
    base = PAIRS + 4
    act_base = base + ACT_DELAY
    steps = [
        (act_base + 4, PAIRS, act_finish),
        (act_base + 3, PAIRS, act_middle2),
        (act_base + 2, PAIRS, act_turn),
        (act_base + 1, PAIRS, act_middle1),
        (base + 4, PAIRS, pre_finish),
        (base + 3, PAIRS, pre_middle2),
        (base + 2, PAIRS, pre_turn),
        (base + 1, PAIRS, pre_middle1),
        (4, 2 * PAIRS, scatter2_finish),
        (3, 2 * PAIRS, scatter2_middle),
        (2, 2 * PAIRS, scatter1_finish),
        (1, 2 * PAIRS, scatter1_middle),
        (0, 2 * PAIRS, multiply),
        (act_base, PAIRS, act_start),
        (base + 4, PAIRS, pre_products),
        (act_base + 4, PAIRS, act_products),
    ]

    def at_ticks(tick, events):
        for when, calls in events.items():

            @pl.when(tick == when)
            def _(calls=calls):
                for call in calls:
                    call()

    @pl.loop(0, TICKS)
    def _(tick):
        at_ticks(tick, early)
        for first, count, step in steps:

            @pl.when((tick >= first) & (tick < first + count))
            def _(first=first, step=step):
                step(tick - first)

        at_ticks(tick, late)

    for p in (PAIRS - 2, PAIRS - 1):
        for order in range(2):
            up_store(p, order).wait()
            down_store(p, order).wait()


def on_device(context, residual, norm_gain, w_out, w_up, w_down, upstream):
    vmem = pl.BlockSpec(memory_space=pltpu.VMEM)
    hbm = pl.BlockSpec(memory_space=pl.ANY)
    shape = jax.ShapeDtypeStruct
    dma = pltpu.SemaphoreType.DMA
    outs = pl.pallas_call(
        kernel,
        out_shape=(
            shape((128, W), BF16),
            shape((64, W), BF16),
            shape((8, W), F32),
            shape((W, W), BF16),
            shape((W, 3072), BF16),
            shape((3072, W), BF16),
        ),
        in_specs=[vmem, vmem, vmem, vmem, hbm, hbm, vmem],
        out_specs=(vmem, vmem, vmem, vmem, hbm, hbm),
        scratch_shapes=[
            pltpu.VMEM((W, 3072), BF16),
            pltpu.VMEM((3072, W), BF16),
            pltpu.VMEM((PAIRS, 2, 4, 4, 64, C), BF16),
            pltpu.VMEM((PAIRS, 2, 6, 2, 64, C), BF16),
            pltpu.VMEM((PAIRS, 2, 6, 32, C), BF16),
            pltpu.VMEM((PAIRS, 2, 64, C), F32),
            pltpu.VMEM((PAIRS, 2, 4, 4, 64, C), BF16),
            pltpu.VMEM((PAIRS, 2, 4, 4, 64, C), BF16),
            pltpu.VMEM((2, 4, 4, 64, CH), BF16),
            pltpu.VMEM((2, 4, 4, 64, CH), BF16),
            pltpu.VMEM((2, 6, 2, 64, CH), BF16),
            pltpu.VMEM((2, 6, 32, CH), BF16),
            pltpu.VMEM((4, 2, 128, W), BF16),
            pltpu.VMEM((4, 2, 128, W), BF16),
            pltpu.VMEM((4, 2, 128, W), BF16),
            pltpu.VMEM((W, 1024), BF16),
            pltpu.VMEM((4, 2, 128, W), F32),
            pltpu.VMEM((4, 2, 128, W), BF16),
            pltpu.VMEM((4, 128, W), BF16),
            pltpu.VMEM((6, 64, W), BF16),
            pltpu.VMEM((2, 4, 8, 128), F32),
            pltpu.VMEM((2, 4, 8, 128), F32),
            pltpu.VMEM((128, W), F32),
            pltpu.VMEM((128, 128), F32),
            pltpu.VMEM((2, 8, W), F32),
            pltpu.VMEM((4, 8, W), F32),
            pltpu.VMEM((2, 2, W, C), BF16),
            pltpu.VMEM((2, 2, C, W), BF16),
            pltpu.VMEM((C, 1024), BF16),
            dma((2,)),
            dma((PAIRS, 2, 6)),
            dma((PAIRS, 2, 6)),
            dma((PAIRS, 2, 6)),
            dma((PAIRS, 2, 6)),
            dma((PAIRS, 2, 8)),
            dma((PAIRS, 2, 8)),
            dma((PAIRS, 2, 8)),
            dma((PAIRS, 2, 8)),
            dma((2, 8)),
            dma((2, 8)),
            dma((2, 6)),
            dma((2, 6)),
            dma((2, 6)),
            dma((2, 6)),
            dma((3, 8)),
            dma((3, 8)),
            dma((7,)),
            dma((7,)),
            dma((2, 6)),
            dma((2, 6)),
            dma((4,)),
            dma((4,)),
            dma((2, 2, 2)),
        ],
        compiler_params=pltpu.CompilerParams(
            collective_id=0, has_side_effects=True, vmem_limit_bytes=63 * 1024 * 1024
        ),
        cost_estimate=pl.CostEstimate(
            flops=28_000_000_000, bytes_accessed=25_000_000, transcendentals=200_000
        ),
    )(context, residual, norm_gain.reshape(1, W), w_out, w_up, w_down, upstream)
    return outs[0], outs[1], outs[2][0], outs[3], outs[4], outs[5]


def solution(mesh):
    return jax.shard_map(
        on_device,
        mesh=mesh,
        in_specs=(
            P("col", "row"),
            P("row", "col"),
            P("col"),
            P("row", "col"),
            P("col", "row"),
            P("row", "col"),
            P("row", "col"),
        ),
        out_specs=(
            P("row", "col"),
            P("col", "row"),
            P("col"),
            P("row", "col"),
            P("col", "row"),
            P("row", "col"),
        ),
        check_vma=False,
    )
```

time: 676 us -> 233 us (0.34)
  waiting for transfers between devices: 461 us -> 0 us
  Pallas kernels: 0 us -> 215 us
  blocking collectives: 131 us -> 0 us
  matrix products: 57.8 us -> 0 us
  local copies, waits for them, and re-layouts: 1.48 us -> 15.4 us
  between operations: 13.9 us -> 0.65 us
  other arithmetic: 9.5 us -> 0.01 us
    reduce_scatter x5 -> x0, waiting for transfers between devices: 271 us -> none  [the longest x1 83.9 us: on_device(): lax.psum_scatter(jnp.dot(normed_all, w_up, preferred_element_type=jnp.flo...]
    pallas_call x0 -> x1, Pallas kernels: none -> 215 us  [on_device(): pl.pallas_call(kernel, out_shape=(shape((128, W), BF16), shape((64, W), B...]
    all_gather x6 -> x0, waiting for transfers between devices: 188 us -> none  [the longest x1 60.7 us: on_device(): grad_pre = lax.all_gather(pre_grad_share, 'col', axis=0, tiled=True)]
    psum x4 -> x0, blocking collectives: 131 us -> none  [the longest x1 40.3 us: on_device(): lax.psum(jnp.sum(summed, axis=1, keepdims=True), 'col') / feature_count]
    dot_general x8 -> x0, matrix products: 57.8 us -> none  [the longest x3 22.6 us: contract_cols(): lax.dot_general(first_op, second_op, (((1,), (1,)), ((), ())), preferred_...]
    unnamed x13 -> x9, local copies, waits for them, and re-layouts: 1.48 us -> 12.8 us
  transfers between devices with their start and end apart: 11 -> 0, of which waited for: 10 -> 0; matrix products, arithmetic and copies ran while one was open for 7% -> 0% of each run, Pallas kernels for 0% -> 0%
where the time goes in v1:
time: 233 us; the launch traced here: 231 us
  Pallas kernels  215 us (92%)
  local copies, waits for them, and re-layouts  15.4 us (7%)
    pallas_call x1, Pallas kernels, on_device(): pl.pallas_call(kernel, out_shape=(shape((128, W), BF16), shape((64, W), B...  215 us
    unnamed x9, local copies, waits for them, and re-layouts  12.8 us

profile of v1, /device:TPU:0, one launch (start us, length us, event | category | flops | bytes accessed | tf_op | source)
XLA Modules:
  0.0 231.2 jit_solution(6640315534272951467)
XLA Ops:
  0.6 1.3 reshape.15.gain_in
  1.9 215.2 %shard_map.118 = (bf16[128,768]{1,0:T(8,128)(2,1)}, bf16[64,768]{1,0:T(8,128)(2,1)}, f32[8,768]{1,0:T(8,128)}, bf16[768,768]{1,0:T(8,128)(2,1)}, bf16[768,3072]{1,0:T(8,128)(2,1)}, /*index=5*/bf16[3072,768]{1,0:T(8,128)(2,1)}) custom-call(bf16[64,768]{1,0:T(8,128)(2,1)} %ctx_in.1, bf16[128,768]{1,0:T(8,128)(2,1)} %res_in.1, f32[1,768]{1,0:T(1,128)} %reshape.15.gain_in, ...), custom_call_target="tpu_custom_call" | custom-call | flops 28000000000 | bytes 25000000 | tf_op jit(solution)/shard_map/pallas_call | solution.py:743
  217.1 1.3 slice_reduce_fusion
  218.4 1.6 copy.18
  220.1 1.5 copy.19
  221.6 0.0 slice-start
  221.6 2.5 %copy.20 = bf16[768,768]{1,0:T(8,128)(2,1)} copy(bf16[768,768]{1,0:T(8,128)(2,1)} %get-tuple-element.27) | data formatting | bytes 2359296
  224.1 0.0 slice-start.1
  224.1 4.9 %copy.21 = bf16[768,3072]{1,0:T(8,128)(2,1)} copy(bf16[768,3072]{1,0:T(8,128)(2,1)} %get-tuple-element.28) | data formatting | bytes 9437184
  229.0 0.0 slice-done
  229.0 0.0 slice-done.1
  229.0 2.2 copy.22
  (1 shorter events, 0.0 us)
Async XLA Ops:
  221.6 7.4 %slice-start = ((s8[4718592]{0:T(1024)(128)(4,1)}), s8[4194304]{0:T(1024)(128)(4,1)S(1)}, s32[]{:S(2)}) async-start(s8[4718592]{0:T(1024)(128)(4,1)} %bitcast), calls=%async_computation | async-start | bytes 8388608
  224.1 4.9 %slice-start.1 = ((s8[4718592]{0:T(1024)(128)(4,1)}), s8[524288]{0:T(1024)(128)(4,1)S(1)}, s32[]{:S(2)}) async-start(s8[4718592]{0:T(1024)(128)(4,1)} %bitcast), calls=%async_computation.1 | async-start | bytes 1048576

commit v2 on v1

--- a/solution.py
+++ b/solution.py
@@ -15,6 +15,7 @@
 CH = 384
 ACT_DELAY = 6
 TICKS = 28
+CUTS = 4
 
 
 def gelu_parts(values):
@@ -128,6 +129,37 @@
     def arrived(self):
         self.copies[2].wait_recv()
         self.copies[3].wait_recv()
+
+    def sent(self):
+        for copy in self.copies:
+            copy.wait_send()
+
+
+class HalfGather:
+    def __init__(self, ring, half, send, recv):
+        r, l, me = ring.right, ring.left, ring.place
+        plan = [(me, 0, r), (me, 1, r), (me, 1, l), (me, 0, l), (l, 0, r), (r, 1, l)]
+
+        def make(k):
+            i, h, to = plan[k]
+            return remote(half(i, h), half(i, h), send.at[k], recv.at[k], ring.device(to))
+
+        self.copies = Copies(make, 6)
+
+    def start(self):
+        for k in (0, 2, 1, 3):
+            self.copies[k].start()
+
+    def middle(self):
+        for first, forward in ((0, 4), (2, 5)):
+            self.copies[first].wait_recv()
+            self.copies[forward].start()
+        for rest in (1, 3):
+            self.copies[rest].wait_recv()
+
+    def arrived(self):
+        self.copies[4].wait_recv()
+        self.copies[5].wait_recv()
 
     def sent(self):
         for copy in self.copies:
@@ -203,6 +235,21 @@
             send.at[pl.ds(4, 4)], recv.at[pl.ds(4, 4)],
         )
 
+    def context_gather1(order):
+        ref, mine = ctx_all.at[order], rings[order].place
+        return HalfGather(
+            rings[1 - order],
+            lambda j, h: block_of(ref, order, mine, j).at[pl.ds(h * 32, 32)],
+            cs.at[order, pl.ds(0, 6)], cv.at[order, pl.ds(0, 6)],
+        )
+
+    def context_gather2(order):
+        return HalfGather(
+            rings[order],
+            lambda i, h: grouped(ctx_all.at[order], order, i, 2 * h, 2),
+            cs.at[order, pl.ds(6, 6)], cv.at[order, pl.ds(6, 6)],
+        )
+
     def scatter_turn(ref, landing, send, recv, order):
         one = scatter1(ref, landing, send, recv, order)
         first, second = one.finish()
@@ -211,17 +258,16 @@
 
     class RowGather:
         def __init__(self, ref, n):
-            self.ring = Gather(
+            self.ring = HalfGather(
                 ring_z,
-                lambda i: ref.at[i, core],
                 lambda i, h: ref.at[i, core, pl.ds(h * 64, 64)],
-                zgs.at[n, pl.ds(0, 4)], zgv.at[n, pl.ds(0, 4)],
+                zgs.at[n, pl.ds(0, 6)], zgv.at[n, pl.ds(0, 6)],
             )
             blocks = (z, ring_z.left, ring_z.right, ring_z.opposite)
             self.near = Copies(
                 lambda k: remote(
                     ref.at[blocks[k], core], ref.at[blocks[k], core],
-                    zgs.at[n, 4 + k], zgv.at[n, 4 + k], sibling,
+                    zgs.at[n, 6 + k], zgv.at[n, 6 + k], sibling,
                 ),
                 4,
             )
@@ -337,13 +383,14 @@
         inv[...] = jnp.broadcast_to(inv_std, (128, 128))
         rows = (unit[...] - to_rows(mean)) * inv_std
         unit[...] = rows
-        normed_all[z, core] = (rows * gain_in[...]).astype(BF16)
+        normed_all[z, core] = (rows * gain_in[...].reshape(1, W)).astype(BF16)
         normed_gather.start()
 
     def normed_done():
         normed_gather.finish()
         load_up.wait()
 
+    def turn_normed():
         @pl.loop(0, 4)
         def _(m):
             for c in range(2):
@@ -372,10 +419,11 @@
         def _():
             for order in range(2):
 
-                @pl.loop(0, 4)
-                def _(m):
-                    value = dot_cols(ups_all[m].reshape(256, W), w_down[columns(i, order), :])
-                    part[slot, order, m] = value.astype(BF16).reshape(4, 64, C)
+                @pl.loop(0, 2)
+                def _(n):
+                    m = pl.ds(n * 2, 2)
+                    value = dot_cols(ups_all[m].reshape(512, W), w_down[columns(i, order), :])
+                    part[slot, order, m] = value.astype(BF16).reshape(2, 4, 64, C)
 
                 scatter1(*unit_scatter1(i, order)).start()
 
@@ -383,10 +431,11 @@
         def _():
             for order in range(2):
 
-                @pl.loop(0, 4)
-                def _(m):
-                    value = dot(normed_all[m].reshape(256, W), w_up[:, columns(i - PAIRS, order)])
-                    part[slot, order, m] = value.astype(BF16).reshape(4, 64, C)
+                @pl.loop(0, 2)
+                def _(n):
+                    m = pl.ds(n * 2, 2)
+                    value = dot(normed_all[m].reshape(512, W), w_up[:, columns(i - PAIRS, order)])
+                    part[slot, order, m] = value.astype(BF16).reshape(2, 4, 64, C)
 
                 scatter1(*unit_scatter1(i, order)).start()
 
@@ -475,7 +524,7 @@
             down_stage.at[slot, order], w_down_out.at[columns(p, order), :], out_sem.at[1, slot, order]
         )
 
-    def pre_products(p):
+    def up_products(p):
         slot = lax.rem(p, 2)
         for order in range(2):
 
@@ -483,14 +532,12 @@
             def _():
                 up_store(p - 2, order).wait()
 
-            @pl.loop(0, 3)
-            def _(n):
-                rows = pl.ds(pl.multiple_of(n * 256, 256), 256)
-                value = dot(normed_t[rows, :], pre_grad[p, order].reshape(1024, C))
-                up_stage[slot, order, rows, :] = value.astype(BF16)
+            value = dot(normed_t[...], pre_grad[p, order].reshape(1024, C))
+            up_stage[slot, order] = value.astype(BF16)
 
             up_store(p, order).start()
 
+    def add_total(p):
         @pl.loop(0, 4)
         def _(m):
             value = dot_cols(pre_grad[p, 0, m].reshape(256, C), w_up[:, columns(p, 0)]) + dot_cols(
@@ -502,9 +549,17 @@
             def _():
                 total[m] = value
 
-            @pl.when(p > 0)
+            @pl.when((p > 0) & (p < PAIRS - 1))
             def _():
                 total[m] += value
+
+            @pl.when(p == PAIRS - 1)
+            def _():
+                z_part[m] = (total[m] + value).astype(BF16)
+
+        @pl.when(p == PAIRS - 1)
+        def _():
+            row_near().start()
 
     def act_products(p):
         slot = lax.rem(p, 2)
@@ -524,10 +579,6 @@
                 down_stage[slot, order, :, cols] = value.astype(BF16)
 
             down_store(p, order).start()
-
-    def reduce_rows():
-        z_part[...] = total[...].astype(BF16)
-        row_near().start()
 
     def gain_near():
         return remote(gain_sib.at[0], gain_sib.at[1], ggs.at[0], ggv.at[0], sibling)
@@ -546,7 +597,7 @@
             total[0, 0, pl.ds(h * 64, 64)] = share
         grad = total[0, 0]
         aligned = grad * unit[...]
-        scaled = grad * gain_in[...]
+        scaled = grad * gain_in[...].reshape(1, W)
         stat_start(
             1, stat_x, ring_x,
             to_lanes(
@@ -571,7 +622,7 @@
     def grad_rows():
         stat_wait(1, stat_y, ring_y)
         means = (stat_y[1, 0] + stat_y[1, 1] + stat_y[1, 2] + stat_y[1, 3]) * (1.0 / D)
-        scaled = total[0, 0] * gain_in[...]
+        scaled = total[0, 0] * gain_in[...].reshape(1, W)
         value = ups_in[...].astype(F32) + inv[:, 0:1] * (
             scaled - to_rows(means[0:1]) - unit[...] * to_rows(means[1:2])
         )
@@ -624,40 +675,45 @@
             for h, share in enumerate(scatter2(*ctx_scatter2(order)).finish()):
                 ctx_out[pl.ds(h * 32, 32), pl.ds(order * CH, CH)] = share.astype(BF16)
 
-    def out_product():
-        for order in range(2):
-            for n in range(3):
-                cols = pl.ds(n * 256, 256)
-                value = lax.dot_general(
-                    ctx_all[order].reshape(1024, CH),
-                    res_all[:, :, :, cols].reshape(1024, 256),
-                    (((0,), (0,)), ((), ())),
-                    preferred_element_type=F32,
-                )
-                w_out_out[pl.ds(order * CH, CH), cols] = value.astype(BF16)
+    def out_product(order):
+        for n in range(3):
+            cols = pl.ds(n * 256, 256)
+            value = lax.dot_general(
+                ctx_all[order].reshape(1024, CH),
+                res_all[:, :, :, cols].reshape(1024, 256),
+                (((0,), (0,)), ((), ())),
+                preferred_element_type=F32,
+            )
+            w_out_out[pl.ds(order * CH, CH), cols] = value.astype(BF16)
+
+    def out_first():
+        out_product(0)
+
+    def out_second():
+        out_product(1)
 
     ups_all[z, core] = ups_in[...]
     ups_gather.start()
     for order in range(2):
         ctx_all[order, x, y] = ctx_in[:, pl.ds(order * CH, CH)]
-        gather1(ctx_all.at[order], cs.at[order], cv.at[order], order).start()
+        context_gather1(order).start()
     for order in range(2):
-        gather1(ctx_all.at[order], cs.at[order], cv.at[order], order).middle()
+        context_gather1(order).middle()
     ups_gather.middle()
     for order in range(2):
-        one = gather1(ctx_all.at[order], cs.at[order], cv.at[order], order)
+        one = context_gather1(order)
         one.arrived()
         one.sent()
-        gather2(ctx_all.at[order], cs.at[order], cv.at[order], order).start()
+        context_gather2(order).start()
     ups_gather.last()
     for order in range(2):
-        gather2(ctx_all.at[order], cs.at[order], cv.at[order], order).middle()
+        context_gather2(order).middle()
     ups_gather.finish()
     load_down.wait()
 
     def context_arrived():
         for order in range(2):
-            one = gather2(ctx_all.at[order], cs.at[order], cv.at[order], order)
+            one = context_gather2(order)
             one.arrived()
             one.sent()
         project_out()
@@ -666,47 +722,48 @@
         1: [row_scatter_ring],
         2: [row_moments],
         3: [normalize],
-        4: [normed_gather.middle],
-        5: [normed_gather.last],
-        6: [normed_done],
+        4: [normed_gather.last],
         20: [row_scatter_ring],
         21: [grad_sums],
         22: [grad_rows],
         23: [res_gather.last],
-        24: [context_middle1],
-        25: [context_turn],
-        26: [context_middle2],
-        27: [context_finish],
     }
     late = {
         0: [context_arrived],
         1: [row_ring.middle],
         2: [moments_x],
-        19: [reduce_rows],
+        3: [normed_gather.middle],
+        5: [normed_done],
+        7: [turn_normed],
         20: [row_ring.middle],
         21: [sums_x],
         22: [gain_done, res_gather.middle],
         23: [context_product],
-        24: [out_product],
+        24: [context_middle1, out_first],
+        25: [context_turn, out_second],
+        26: [context_middle2],
+        27: [context_finish],
     }
     base = PAIRS + 4
     act_base = base + ACT_DELAY
     steps = [
+        (0, 2 * PAIRS, multiply),
+        (1, 2 * PAIRS, scatter1_middle),
+        (2, 2 * PAIRS, scatter1_finish),
+        (3, 2 * PAIRS, scatter2_middle),
+        (4, 2 * PAIRS, scatter2_finish),
+        (base + 1, PAIRS, pre_middle1),
+        (base + 2, PAIRS, pre_turn),
+        (base + 3, PAIRS, pre_middle2),
+        (base + 4, PAIRS, pre_finish),
+        (base + 4, PAIRS, add_total),
+        (act_base, PAIRS, act_start),
+        (act_base + 1, PAIRS, act_middle1),
+        (act_base + 2, PAIRS, act_turn),
+        (act_base + 3, PAIRS, act_middle2),
         (act_base + 4, PAIRS, act_finish),
-        (act_base + 3, PAIRS, act_middle2),
-        (act_base + 2, PAIRS, act_turn),
-        (act_base + 1, PAIRS, act_middle1),
-        (base + 4, PAIRS, pre_finish),
-        (base + 3, PAIRS, pre_middle2),
-        (base + 2, PAIRS, pre_turn),
-        (base + 1, PAIRS, pre_middle1),
-        (4, 2 * PAIRS, scatter2_finish),
-        (3, 2 * PAIRS, scatter2_middle),
-        (2, 2 * PAIRS, scatter1_finish),
-        (1, 2 * PAIRS, scatter1_middle),
-        (0, 2 * PAIRS, multiply),
-        (act_base, PAIRS, act_start),
-        (base + 4, PAIRS, pre_products),
+        None,
+        (base + 4, PAIRS, up_products),
         (act_base + 4, PAIRS, act_products),
     ]
 
@@ -720,8 +777,11 @@
 
     @pl.loop(0, TICKS)
     def _(tick):
-        at_ticks(tick, early)
-        for first, count, step in steps:
+        for entry in steps:
+            if entry is None:
+                at_ticks(tick, early)
+                continue
+            first, count, step = entry
 
             @pl.when((tick >= first) & (tick < first + count))
             def _(first=first, step=step):
@@ -791,14 +851,14 @@
             dma((PAIRS, 2, 8)),
             dma((PAIRS, 2, 8)),
             dma((PAIRS, 2, 8)),
-            dma((2, 8)),
-            dma((2, 8)),
+            dma((2, 12)),
+            dma((2, 12)),
             dma((2, 6)),
             dma((2, 6)),
             dma((2, 6)),
             dma((2, 6)),
-            dma((3, 8)),
-            dma((3, 8)),
+            dma((3, 10)),
+            dma((3, 10)),
             dma((7,)),
             dma((7,)),
             dma((2, 6)),
@@ -813,8 +873,47 @@
         cost_estimate=pl.CostEstimate(
             flops=28_000_000_000, bytes_accessed=25_000_000, transcendentals=200_000
         ),
-    )(context, residual, norm_gain.reshape(1, W), w_out, w_up, w_down, upstream)
-    return outs[0], outs[1], outs[2][0], outs[3], outs[4], outs[5]
+    )(context, residual, norm_gain, w_out, w_up, w_down, upstream)
+    return hand_over(outs)
+
+
+def copy_kernel(*refs):
+    ends, held, sems = refs[:10], refs[10:15], refs[15]
+    parts = []
+    for src, via, dst in zip(ends[:5], held, ends[5:]):
+        rows = src.shape[0] // CUTS
+        parts += [(src, via, dst, pl.ds(n * rows, rows)) for n in range(CUTS)]
+    reads = [
+        pltpu.make_async_copy(src.at[part], via.at[part], sems.at[0, n])
+        for n, (src, via, _, part) in enumerate(parts)
+    ]
+    writes = [
+        pltpu.make_async_copy(via.at[part], dst.at[part], sems.at[1, n])
+        for n, (_, via, dst, part) in enumerate(parts)
+    ]
+    for copy in reads:
+        copy.start()
+    for n, copy in enumerate(writes):
+        reads[n].wait()
+        copy.start()
+    for copy in writes:
+        copy.wait()
+
+
+def hand_over(outs):
+    moved = [outs[n] for n in (0, 1, 3, 4, 5)]
+    hbm = pl.BlockSpec(memory_space=pl.ANY)
+    a, b, d, e, f = pl.pallas_call(
+        copy_kernel,
+        out_shape=[jax.ShapeDtypeStruct(ref.shape, ref.dtype) for ref in moved],
+        in_specs=[hbm] * 5,
+        out_specs=[hbm] * 5,
+        scratch_shapes=[pltpu.VMEM(ref.shape, ref.dtype) for ref in moved]
+        + [pltpu.SemaphoreType.DMA((2, 5 * CUTS))],
+        compiler_params=pltpu.CompilerParams(vmem_limit_bytes=48 * 1024 * 1024),
+        cost_estimate=pl.CostEstimate(flops=0, bytes_accessed=22_000_000, transcendentals=0),
+    )(*moved)
+    return a, b, outs[2][0], d, e, f
 
 
 def solution(mesh):

time: 233 us -> 220 us (0.944)
  local copies, waits for them, and re-layouts: 15.4 us -> 6.76 us
  Pallas kernels: 215 us -> 212 us
    pallas_call x1, Pallas kernels: 215 us -> 204 us  [on_device(): pl.pallas_call(kernel, out_shape=(shape((128, W), BF16), shape((64, W), B...]
    pallas_call x0 -> x1, Pallas kernels: none -> 8.23 us  [hand_over(): pl.pallas_call(copy_kernel, out_shape=[jax.ShapeDtypeStruct(ref.shape, re...]
    unnamed x9 -> x8, local copies, waits for them, and re-layouts: 12.8 us -> 5.42 us
where the time goes in v2:
time: 220 us
  Pallas kernels  212 us (96%)
  local copies, waits for them, and re-layouts  6.76 us (3%)
    pallas_call x1, Pallas kernels, on_device(): pl.pallas_call(kernel, out_shape=(shape((128, W), BF16), shape((64, W), B...  204 us
    pallas_call x1, Pallas kernels, hand_over(): pl.pallas_call(copy_kernel, out_shape=[jax.ShapeDtypeStruct(ref.shape, re...  8.23 us
    unnamed x8, local copies, waits for them, and re-layouts  5.42 us

profile of v2, /device:TPU:0, one launch (start us, length us, event | category | flops | bytes accessed | tf_op | source)
XLA Modules:
  0.0 219.8 jit_solution(9695326335876486423)
XLA Ops:
  0.6 204.1 %shard_map.118 = (bf16[128,768]{1,0:T(8,128)(2,1)}, bf16[64,768]{1,0:T(8,128)(2,1)}, f32[8,768]{1,0:T(8,128)}, bf16[768,768]{1,0:T(8,128)(2,1)}, bf16[768,3072]{1,0:T(8,128)(2,1)}, /*index=5*/bf16[3072,768]{1,0:T(8,128)(2,1)}) custom-call(bf16[64,768]{1,0:T(8,128)(2,1)} %ctx_in.1, bf16[128,768]{1,0:T(8,128)(2,1)} %res_in.1, f32[768]{0:T(1024)} %gain_in.1, ...), custom_call_target="tpu_custom_call" | custom-call | flops 28000000000 | bytes 25000000 | tf_op jit(solution)/shard_map/pallas_call | solution.py:803
  204.8 0.0 copy-start
  204.8 2.3 %copy-done = bf16[768,3072]{1,0:T(8,128)(2,1)S(1)} copy-done((bf16[768,3072]{1,0:T(8,128)(2,1)S(1)}, bf16[768,3072]{1,0:T(8,128)(2,1)}, u32[]{:S(2)}) %copy-start) | copy-done | bytes 4718616
  207.1 0.0 copy-start.1
  207.1 1.3 copy-done.1
  208.4 0.0 copy-start.2
  208.4 0.9 copy-done.2
  209.3 0.0 copy-start.3
  209.3 0.9 copy-done.3
  210.2 8.2 %shard_map.119 = (bf16[128,768]{1,0:T(8,128)(2,1)}, bf16[64,768]{1,0:T(8,128)(2,1)}, bf16[768,768]{1,0:T(8,128)(2,1)}, bf16[768,3072]{1,0:T(8,128)(2,1)}, bf16[3072,768]{1,0:T(8,128)(2,1)}) custom-call(bf16[128,768]{1,0:T(8,128)(2,1)S(1)} %copy-done.2, bf16[64,768]{1,0:T(8,128)(2,1)S(1)} %copy-done.3, bf16[768,768]{1,0:T(8,128)(2,1)S(1)} %copy-done.1, ...), custom_call_target="tpu_custom_call" | custom-call | bytes 22000000 | tf_op jit(solution)/shard_map/pallas_call | solution.py:906
  218.5 1.3 slice_reduce_fusion
Async XLA Ops:
  204.8 2.3 %copy-start = (bf16[768,3072]{1,0:T(8,128)(2,1)S(1)}, bf16[768,3072]{1,0:T(8,128)(2,1)}, u32[]{:S(2)}) copy-start(bf16[768,3072]{1,0:T(8,128)(2,1)} %get-tuple-element.20.refs_3_) | copy-start | bytes 14155780
  207.1 1.3 copy-start.1
  208.4 0.9 copy-start.2
  209.3 0.9 copy-start.3

commit v3 on v2

--- a/solution.py
+++ b/solution.py
@@ -910,7 +910,7 @@
         out_specs=[hbm] * 5,
         scratch_shapes=[pltpu.VMEM(ref.shape, ref.dtype) for ref in moved]
         + [pltpu.SemaphoreType.DMA((2, 5 * CUTS))],
-        compiler_params=pltpu.CompilerParams(vmem_limit_bytes=48 * 1024 * 1024),
+        compiler_params=pltpu.CompilerParams(vmem_limit_bytes=63 * 1024 * 1024),
         cost_estimate=pl.CostEstimate(flops=0, bytes_accessed=22_000_000, transcendentals=0),
     )(*moved)
     return a, b, outs[2][0], d, e, f

time: 220 us -> 215 us (0.977)
  local copies, waits for them, and re-layouts: 6.76 us -> 1.34 us
    unnamed x8 -> x0, local copies, waits for them, and re-layouts: 5.42 us -> none
where the time goes in v3:
time: 215 us
  Pallas kernels  213 us (99%)
    pallas_call x1, Pallas kernels, on_device(): pl.pallas_call(kernel, out_shape=(shape((128, W), BF16), shape((64, W), B...  204 us
    pallas_call x1, Pallas kernels, hand_over(): pl.pallas_call(copy_kernel, out_shape=[jax.ShapeDtypeStruct(ref.shape, re...  8.58 us

profile of v3, /device:TPU:0, one launch (start us, length us, event | category | flops | bytes accessed | tf_op | source)
XLA Modules:
  0.0 214.7 jit_solution(13279741860188778770)
XLA Ops:
  0.6 204.1 %shard_map.118 = (bf16[128,768]{1,0:T(8,128)(2,1)}, bf16[64,768]{1,0:T(8,128)(2,1)}, f32[8,768]{1,0:T(8,128)}, bf16[768,768]{1,0:T(8,128)(2,1)}, bf16[768,3072]{1,0:T(8,128)(2,1)}, /*index=5*/bf16[3072,768]{1,0:T(8,128)(2,1)}) custom-call(bf16[64,768]{1,0:T(8,128)(2,1)} %ctx_in.1, bf16[128,768]{1,0:T(8,128)(2,1)} %res_in.1, f32[768]{0:T(1024)} %gain_in.1, ...), custom_call_target="tpu_custom_call" | custom-call | flops 28000000000 | bytes 25000000 | tf_op jit(solution)/shard_map/pallas_call | solution.py:803
  204.8 8.6 %shard_map.119 = (bf16[128,768]{1,0:T(8,128)(2,1)}, bf16[64,768]{1,0:T(8,128)(2,1)}, bf16[768,768]{1,0:T(8,128)(2,1)}, bf16[768,3072]{1,0:T(8,128)(2,1)}, bf16[3072,768]{1,0:T(8,128)(2,1)}) custom-call(bf16[128,768]{1,0:T(8,128)(2,1)} %get-tuple-element.17.refs_0_, bf16[64,768]{1,0:T(8,128)(2,1)} %get-tuple-element.18.refs_1_, ...), custom_call_target="tpu_custom_call" | custom-call | bytes 22000000 | tf_op jit(solution)/shard_map/pallas_call | solution.py:906
  213.3 1.3 slice_reduce_fusion

commit v4 on v3

--- a/solution.py
+++ b/solution.py
@@ -878,7 +878,7 @@
 
 
 def copy_kernel(*refs):
-    ends, held, sems = refs[:10], refs[10:15], refs[15]
+    ends, gain, held, sems = refs[:5] + refs[6:11], (refs[5], refs[11]), refs[12:17], refs[17]
     parts = []
     for src, via, dst in zip(ends[:5], held, ends[5:]):
         rows = src.shape[0] // CUTS
@@ -893,6 +893,7 @@
     ]
     for copy in reads:
         copy.start()
+    gain[1][...] = gain[0][0:1, :].reshape(W)
     for n, copy in enumerate(writes):
         reads[n].wait()
         copy.start()
@@ -903,17 +904,19 @@
 def hand_over(outs):
     moved = [outs[n] for n in (0, 1, 3, 4, 5)]
     hbm = pl.BlockSpec(memory_space=pl.ANY)
-    a, b, d, e, f = pl.pallas_call(
+    vmem = pl.BlockSpec(memory_space=pltpu.VMEM)
+    a, b, d, e, f, gain = pl.pallas_call(
         copy_kernel,
-        out_shape=[jax.ShapeDtypeStruct(ref.shape, ref.dtype) for ref in moved],
-        in_specs=[hbm] * 5,
-        out_specs=[hbm] * 5,
+        out_shape=[jax.ShapeDtypeStruct(ref.shape, ref.dtype) for ref in moved]
+        + [jax.ShapeDtypeStruct((W,), F32)],
+        in_specs=[hbm] * 5 + [vmem],
+        out_specs=[hbm] * 5 + [vmem],
         scratch_shapes=[pltpu.VMEM(ref.shape, ref.dtype) for ref in moved]
         + [pltpu.SemaphoreType.DMA((2, 5 * CUTS))],
         compiler_params=pltpu.CompilerParams(vmem_limit_bytes=63 * 1024 * 1024),
         cost_estimate=pl.CostEstimate(flops=0, bytes_accessed=22_000_000, transcendentals=0),
-    )(*moved)
-    return a, b, outs[2][0], d, e, f
+    )(*moved, outs[2])
+    return a, b, gain, d, e, f
 
 
 def solution(mesh):

time: 215 us -> 215 us (level)
  no operation moved by 1% of the time
where the time goes in v4:
time: 215 us
  Pallas kernels  214 us (100%)
    pallas_call x1, Pallas kernels, on_device(): pl.pallas_call(kernel, out_shape=(shape((128, W), BF16), shape((64, W), B...  204 us
    pallas_call x1, Pallas kernels, hand_over(): pl.pallas_call(copy_kernel, out_shape=[jax.ShapeDtypeStruct(ref.shape, re...  9.89 us

profile of v4, /device:TPU:0, one launch (start us, length us, event | category | flops | bytes accessed | tf_op | source)
XLA Modules:
  0.0 214.7 jit_solution(1670368202611455861)
XLA Ops:
  0.6 204.1 %shard_map.118 = (bf16[128,768]{1,0:T(8,128)(2,1)}, bf16[64,768]{1,0:T(8,128)(2,1)}, f32[8,768]{1,0:T(8,128)}, bf16[768,768]{1,0:T(8,128)(2,1)}, bf16[768,3072]{1,0:T(8,128)(2,1)}, /*index=5*/bf16[3072,768]{1,0:T(8,128)(2,1)}) custom-call(bf16[64,768]{1,0:T(8,128)(2,1)} %ctx_in.1, bf16[128,768]{1,0:T(8,128)(2,1)} %res_in.1, f32[768]{0:T(1024)} %gain_in.1, ...), custom_call_target="tpu_custom_call" | custom-call | flops 28000000000 | bytes 25000000 | tf_op jit(solution)/shard_map/pallas_call | solution.py:803
  204.8 9.9 %shard_map.119 = (bf16[128,768]{1,0:T(8,128)(2,1)}, bf16[64,768]{1,0:T(8,128)(2,1)}, bf16[768,768]{1,0:T(8,128)(2,1)}, bf16[768,3072]{1,0:T(8,128)(2,1)}, bf16[3072,768]{1,0:T(8,128)(2,1)}, /*index=5*/f32[768]{0:T(1024)}) custom-call(bf16[128,768]{1,0:T(8,128)(2,1)} %get-tuple-element.18.refs_0_, bf16[64,768]{1,0:T(8,128)(2,1)} %get-tuple-element.19.refs_1_, ...), custom_call_target="tpu_custom_call" | custom-call | bytes 22000000 | tf_op jit(solution)/shard_map/pallas_call | solution.py:908
